TPU v7x, 32 devices: a whole 2x2x4 slice. The times are simulated.
32 devices in a mesh: clip: 8 (over z, x), frame: 4 (over y, core).
Axes of the slice: x: 2, y: 2, z: 4, core: 2. Of those that a mesh axis runs over, the one named last changes fastest.
Arguments:
- media: bfloat16 [16, 4, 256, 1536], P('clip', 'frame'), may hold values from -6 to 6
- frame_order: int32 [16, 4], P('clip'), may hold values from 0 to 3, each once within a row
- clip_counts: int32 [4], replicated, may hold values from 1 to 4, as said below
- latents: float32 [16, 64, 1536], P('clip'), may hold values from -6 to 6
- time_embed: float32 [4, 1536], replicated, may hold values from -6 to 6
- media_gain: float32 [2, 1536], replicated, may hold values from 0.25 to 1.75
- latent_gain: float32 [2, 1536], replicated, may hold values from 0.25 to 1.75
- ffn_gain: float32 [2, 1536], replicated, may hold values from 0.25 to 1.75
- query_weight: bfloat16 [2, 1536, 1536], P(None, None, 'frame'), may hold values from -0.15625 to 0.15625
- key_weight: bfloat16 [2, 1536, 1536], P(None, None, 'frame'), may hold values from -0.15625 to 0.15625
- value_weight: bfloat16 [2, 1536, 1536], P(None, None, 'frame'), may hold values from -0.15625 to 0.15625
- out_weight: bfloat16 [2, 1536, 1536], P(None, 'frame'), may hold values from -2.5 to 2.5
- up_weight: bfloat16 [2, 1536, 6144], P(None, None, 'frame'), may hold values from -0.15625 to 0.15625
- down_weight: bfloat16 [2, 6144, 1536], P(None, 'frame'), may hold values from -0.078125 to 0.078125
- cotangent: float32 [16, 64, 1536], P('clip'), may hold values from -6 to 6
Outputs:
- latents_out: float32 [16, 64, 1536], P('clip')
- media_grad: float32 [16, 4, 256, 1536], P('clip', 'frame')
- latents_grad: float32 [16, 64, 1536], P('clip')
- time_grad: float32 [4, 1536], P(None, ('clip', 'frame'))
- media_gain_grad: float32 [2, 1536], P(None, ('clip', 'frame'))
- latent_gain_grad: float32 [2, 1536], P(None, 'clip')
- ffn_gain_grad: float32 [2, 1536], P(None, 'clip')
- query_weight_grad: float32 [2, 1536, 1536], P(None, 'clip', 'frame')
- key_weight_grad: float32 [2, 1536, 1536], P(None, 'clip', 'frame')
- value_weight_grad: float32 [2, 1536, 1536], P(None, 'clip', 'frame')
- out_weight_grad: float32 [2, 1536, 1536], P(None, 'frame', 'clip')
- up_weight_grad: float32 [2, 1536, 6144], P(None, 'clip', 'frame')
- down_weight_grad: float32 [2, 6144, 1536], P(None, 'frame', 'clip')
Inputs may be any that keep to these rules, and one draw needn't show every extreme that they name: `clip_counts`: every sequence has at least one live clip, and some sequence fills all 4 slots. `frame_order`: each clip's row is a permutation of the 4 time positions.
All inputs are finite; a program needn't handle non-finite values.
Results may differ from a plain program's by a relative error of at most 0.028.
Values may be sent and summed in bfloat16 or wider, within the bound.
No kernel may reach another device: no remote copies, remote signals or barrier semaphores. Data moves between devices by JAX's collectives and lax.ppermute only.
A program may use at most 256 MiB of HBM per device.

v0:
```python
import jax
import jax.numpy as jnp
from jax import lax
from jax.sharding import PartitionSpec as P

HEADS = 16
HEAD_DIM = 96
LATENTS = 64
LAYERS = 2
SLOTS = 4


EPSILON = 1e-05
HIGHEST = lax.Precision.HIGHEST


def norm_plain(values_in):
    row_mean = jnp.mean(values_in, axis=-1, keepdims=True)
    centred = values_in - row_mean
    inverse = lax.rsqrt(jnp.mean(centred * centred, axis=-1, keepdims=True) + EPSILON)
    return (centred * inverse, inverse)


def norm_back(grad_in, normed, inverse):
    grad_mean = jnp.mean(grad_in, axis=-1, keepdims=True)
    along = jnp.mean(grad_in * normed, axis=-1, keepdims=True)
    return inverse * (grad_in - grad_mean - normed * along)


def product(left_op, right_op):
    return jnp.dot(left_op, right_op, preferred_element_type=jnp.float32)


def latent_sums(partial_sum):
    return lax.psum(partial_sum.astype(jnp.bfloat16), "frame").astype(jnp.float32)


def latent_grads(partial_sum):
    return lax.psum(partial_sum.astype(jnp.bfloat16), "frame").astype(jnp.float32)


def exact_gelu(pre_act):
    return jax.nn.gelu(pre_act, approximate=False)


def block_layout(stacked, clip_total, frame_total):
    layer_total, row_total, col_total = stacked.shape
    blocks = stacked.reshape(
        layer_total, clip_total, row_total // clip_total, frame_total, col_total // frame_total
    )
    blocks = jnp.transpose(blocks, (0, 1, 3, 2, 4))
    return blocks.reshape(layer_total, row_total * frame_total, col_total // frame_total)


def on_device(
    media,
    frame_order,
    clip_counts,
    latents,
    time_embed,
    media_gain,
    latent_gain,
    ffn_gain,
    query_weight,
    key_weight,
    value_weight,
    out_weight,
    up_weight,
    down_weight,
    cotangent,
):
    clip_count = media.shape[0]
    width_all = media.shape[3]
    frame_count = lax.axis_size("frame")
    clip_total = lax.axis_size("clip")
    frame_here = lax.axis_index("frame")
    row_count = LATENTS // frame_count
    row_start = frame_here * row_count
    scaling = HEAD_DIM ** (-0.5)
    f32 = jnp.float32
    bf16 = jnp.bfloat16
    order_own = lax.dynamic_slice_in_dim(frame_order, frame_here, 1, 1)[:, 0]
    onehot = (order_own[:, None] == jnp.arange(frame_count, dtype=jnp.int32)[None, :]).astype(f32)
    stamped = media[:, 0].astype(f32) + jnp.dot(onehot, time_embed, precision=HIGHEST)[:, None, :]
    media_plain, media_inv = norm_plain(stamped)
    media_rows = media_plain.shape[1]
    clip_ids = lax.axis_index("clip") * clip_count + jnp.arange(clip_count, dtype=jnp.int32)
    owner_match = (clip_ids // SLOTS)[:, None] == jnp.arange(clip_counts.shape[0], dtype=jnp.int32)[
        None, :
    ]
    owner_count = jnp.sum(jnp.where(owner_match, clip_counts[None, :], 0), axis=1)
    living = (clip_ids % SLOTS < owner_count).astype(f32)[:, None, None]
    stored = []
    current = latents
    for layer_no in range(LAYERS):
        media_n = (media_plain * media_gain[layer_no]).astype(bf16)
        latent_plain, latent_inv = norm_plain(current)
        latent_n = (latent_plain * latent_gain[layer_no]).astype(bf16)
        key_full, value_full = (
            lax.all_gather(key_weight[layer_no], "frame", axis=1, tiled=True),
            lax.all_gather(value_weight[layer_no], "frame", axis=1, tiled=True),
        )
        own_rows = lax.dynamic_slice_in_dim(latent_n, row_start, row_count, 1)
        sources = jnp.concatenate([media_n, own_rows], axis=1)
        keys_all = product(sources, key_full).astype(bf16).reshape(clip_count, -1, HEADS, HEAD_DIM)
        values_all = (
            product(sources, value_full).astype(bf16).reshape(clip_count, -1, HEADS, HEAD_DIM)
        )
        query_own = product(latent_n, query_weight[layer_no]).astype(bf16)
        queries = lax.all_gather(query_own, "frame", axis=2, tiled=True).reshape(
            clip_count, LATENTS, HEADS, HEAD_DIM
        )
        scores = (
            jnp.einsum("cqhd,ckhd->chqk", queries, keys_all, preferred_element_type=f32) * scaling
        )
        top_score = lax.pmax(jnp.max(scores, axis=3), "frame")
        score_sum = lax.psum(jnp.sum(jnp.exp(scores - top_score[..., None]), axis=3), "frame")
        soft_weights = jnp.exp(scores - top_score[..., None]) / score_sum[..., None]
        partial_out = jnp.einsum(
            "chqk,ckhd->cqhd", soft_weights.astype(bf16), values_all, preferred_element_type=f32
        ).reshape(clip_count, LATENTS, width_all)
        attended = (
            lax.psum_scatter(
                partial_out.astype(jnp.bfloat16), "frame", scatter_dimension=2, tiled=True
            )
            .astype(jnp.float32)
            .astype(bf16)
        )
        middle = current + latent_sums(product(attended, out_weight[layer_no]))
        ffn_plain, ffn_inv = norm_plain(middle)
        ffn_in = (ffn_plain * ffn_gain[layer_no]).astype(bf16)
        pre_act = product(ffn_in, up_weight[layer_no])
        hidden = exact_gelu(pre_act).astype(bf16)
        current = middle + latent_sums(product(hidden, down_weight[layer_no]))
        stored.append(
            (
                key_full,
                value_full,
                latent_plain,
                latent_inv,
                latent_n,
                sources,
                keys_all,
                values_all,
                queries,
                top_score,
                score_sum,
                attended,
                ffn_plain,
                ffn_inv,
                ffn_in,
                pre_act,
                hidden,
            )
        )
    latents_out = current * living
    grad_now = cotangent * living
    grad_stamped = jnp.zeros_like(media_plain)
    key_grads, value_grads, query_grads, out_grads, up_grads, down_grads = ([], [], [], [], [], [])
    media_gain_grads, latent_gain_grads, ffn_gain_grads = ([], [], [])
    for layer_no in reversed(range(LAYERS)):
        (
            key_full,
            value_full,
            latent_plain,
            latent_inv,
            latent_n,
            sources,
            keys_all,
            values_all,
            queries,
            top_score,
            score_sum,
            attended,
            ffn_plain,
            ffn_inv,
            ffn_in,
            pre_act,
            hidden,
        ) = stored[layer_no]
        grad_branch = grad_now.astype(bf16)
        grad_hidden = jnp.einsum(
            "cld,fd->clf", grad_branch, down_weight[layer_no], preferred_element_type=f32
        )
        gelu_pull = jax.vjp(exact_gelu, pre_act)[1]
        grad_pre = gelu_pull(grad_hidden)[0].astype(bf16)
        down_grads.append(
            jnp.einsum("clf,cld->fd", hidden, grad_branch, preferred_element_type=f32)
        )
        up_grads.append(jnp.einsum("cld,clf->df", ffn_in, grad_pre, preferred_element_type=f32))
        grad_ffn = latent_grads(
            jnp.einsum("clf,df->cld", grad_pre, up_weight[layer_no], preferred_element_type=f32)
        )
        ffn_gain_grads.append(jnp.sum(grad_ffn * ffn_plain, axis=(0, 1)))
        grad_middle = grad_now + norm_back(grad_ffn * ffn_gain[layer_no], ffn_plain, ffn_inv)
        grad_update = grad_middle.astype(bf16)
        out_grads.append(
            jnp.einsum("clh,cld->hd", attended, grad_update, preferred_element_type=f32)
        )
        grad_att_own = jnp.einsum(
            "cld,hd->clh", grad_update, out_weight[layer_no], preferred_element_type=f32
        ).astype(bf16)
        grad_att = lax.all_gather(grad_att_own, "frame", axis=2, tiled=True).reshape(
            clip_count, LATENTS, HEADS, HEAD_DIM
        )
        scores = (
            jnp.einsum("cqhd,ckhd->chqk", queries, keys_all, preferred_element_type=f32) * scaling
        )
        soft_weights = jnp.exp(scores - top_score[..., None]) / score_sum[..., None]
        grad_soft = jnp.einsum("cqhd,ckhd->chqk", grad_att, values_all, preferred_element_type=f32)
        local_delta = jnp.sum(soft_weights * grad_soft, axis=3)
        delta_sum = lax.psum(local_delta, "frame")
        grad_scores = (soft_weights * (grad_soft - delta_sum[..., None])).astype(bf16)
        grad_query_all = (
            jnp.einsum(
                "chqk,ckhd->cqhd", grad_scores, keys_all, preferred_element_type=f32
            ).reshape(clip_count, LATENTS, -1)
            * scaling
        )
        grad_query = (
            lax.psum_scatter(
                grad_query_all.astype(jnp.bfloat16), "frame", scatter_dimension=2, tiled=True
            )
            .astype(jnp.float32)
            .astype(bf16)
        )
        grad_keys = (
            (
                jnp.einsum("chqk,cqhd->ckhd", grad_scores, queries, preferred_element_type=f32)
                * scaling
            )
            .reshape(clip_count, keys_all.shape[1], -1)
            .astype(bf16)
        )
        grad_values = (
            jnp.einsum(
                "chqk,cqhd->ckhd", soft_weights.astype(bf16), grad_att, preferred_element_type=f32
            )
            .reshape(clip_count, keys_all.shape[1], -1)
            .astype(bf16)
        )
        key_grads.append(jnp.einsum("ckd,cke->de", sources, grad_keys, preferred_element_type=f32))
        value_grads.append(
            jnp.einsum("ckd,cke->de", sources, grad_values, preferred_element_type=f32)
        )
        query_grads.append(
            jnp.einsum("cld,clh->dh", latent_n, grad_query, preferred_element_type=f32)
        )
        key_full, value_full = (
            lax.all_gather(key_weight[layer_no], "frame", axis=1, tiled=True),
            lax.all_gather(value_weight[layer_no], "frame", axis=1, tiled=True),
        )
        grad_sources = jnp.einsum(
            "cke,de->ckd", grad_keys, key_full, preferred_element_type=f32
        ) + jnp.einsum("cke,de->ckd", grad_values, value_full, preferred_element_type=f32)
        grad_media_n = grad_sources[:, :media_rows]
        grad_rows = grad_sources[:, media_rows:]
        grad_latent_part = jnp.einsum(
            "clh,dh->cld", grad_query, query_weight[layer_no], preferred_element_type=f32
        )
        grad_latent_part = grad_latent_part + lax.dynamic_update_slice_in_dim(
            jnp.zeros_like(grad_latent_part), grad_rows, row_start, 1
        )
        grad_latent = latent_grads(grad_latent_part)
        latent_gain_grads.append(jnp.sum(grad_latent * latent_plain, axis=(0, 1)))
        grad_now = grad_middle + norm_back(
            grad_latent * latent_gain[layer_no], latent_plain, latent_inv
        )
        media_gain_grads.append(jnp.sum(grad_media_n * media_plain, axis=(0, 1)))
        grad_stamped = grad_stamped + norm_back(
            grad_media_n * media_gain[layer_no], media_plain, media_inv
        )
    key_stack = jnp.stack(key_grads[::-1])
    value_stack = jnp.stack(value_grads[::-1])
    time_grad = jnp.dot(onehot.T, jnp.sum(grad_stamped, axis=1), precision=HIGHEST)
    media_grad = grad_stamped[:, None]
    key_all, value_all, media_gain_all, time_all = (
        lax.psum_scatter(
            block_layout(key_stack, clip_total, frame_count),
            ("clip", "frame"),
            scatter_dimension=1,
            tiled=True,
        ),
        lax.psum_scatter(
            block_layout(value_stack, clip_total, frame_count),
            ("clip", "frame"),
            scatter_dimension=1,
            tiled=True,
        ),
        lax.psum_scatter(
            jnp.stack(media_gain_grads[::-1]), ("clip", "frame"), scatter_dimension=1, tiled=True
        ),
        lax.psum_scatter(time_grad, ("clip", "frame"), scatter_dimension=1, tiled=True),
    )
    query_part, out_part, up_part, down_part, latent_gain_part, ffn_gain_part = (
        lax.psum_scatter(
            jnp.stack(query_grads[::-1]).astype(jnp.bfloat16),
            "clip",
            scatter_dimension=1,
            tiled=True,
        ).astype(jnp.float32),
        lax.psum_scatter(
            jnp.stack(out_grads[::-1]).astype(jnp.bfloat16), "clip", scatter_dimension=2, tiled=True
        ).astype(jnp.float32),
        lax.psum_scatter(
            jnp.stack(up_grads[::-1]).astype(jnp.bfloat16), "clip", scatter_dimension=1, tiled=True
        ).astype(jnp.float32),
        lax.psum_scatter(
            jnp.stack(down_grads[::-1]).astype(jnp.bfloat16),
            "clip",
            scatter_dimension=2,
            tiled=True,
        ).astype(jnp.float32),
        lax.psum_scatter(
            jnp.stack(latent_gain_grads[::-1]).astype(jnp.bfloat16),
            "clip",
            scatter_dimension=1,
            tiled=True,
        ).astype(jnp.float32),
        lax.psum_scatter(
            jnp.stack(ffn_gain_grads[::-1]).astype(jnp.bfloat16),
            "clip",
            scatter_dimension=1,
            tiled=True,
        ).astype(jnp.float32),
    )
    return (
        latents_out,
        media_grad,
        grad_now,
        time_all,
        media_gain_all,
        latent_gain_part,
        ffn_gain_part,
        query_part,
        key_all,
        value_all,
        out_part,
        up_part,
        down_part,
    )


def solution(mesh):
    return jax.shard_map(
        on_device,
        mesh=mesh,
        in_specs=(
            P("clip", "frame", None, None),
            P("clip", None),
            P(),
            P("clip", None, None),
            P(),
            P(),
            P(),
            P(),
            P(None, None, "frame"),
            P(None, None, "frame"),
            P(None, None, "frame"),
            P(None, "frame", None),
            P(None, None, "frame"),
            P(None, "frame", None),
            P("clip", None, None),
        ),
        out_specs=(
            P("clip", None, None),
            P("clip", "frame", None, None),
            P("clip", None, None),
            P(None, ("clip", "frame")),
            P(None, ("clip", "frame")),
            P(None, "clip"),
            P(None, "clip"),
            P(None, "clip", "frame"),
            P(None, "clip", "frame"),
            P(None, "clip", "frame"),
            P(None, "frame", "clip"),
            P(None, "clip", "frame"),
            P(None, "frame", "clip"),
        ),
        check_vma=False,
    )
```

profile of v0, /device:TPU:0, one launch (start us, length us, event | category | flops | bytes accessed | tf_op | source)
XLA Modules:
  0.0 2107.9 jit_solution(15337915588366069265)
XLA Ops:
  15.3 7.9 all_gather.29
  28.6 22.3 %all-gather.9.cloned.1.call-done = bf16[1,1536,1536]{2,1,0:T(8,128)(2,1)} async-done(((bf16[1,1536,384]{2,1,0:T(8,128)(2,1)}), bf16[1,1536,1536]{2,1,0:T(8,128)(2,1)}) %all-gather.9.cloned.1.call-update) | async-done | bytes 4718608 | tf_op jit(solution)/shard_map/all_gather | solution.py:101
  62.4 28.1 %all-gather.11.cloned.1.call-done = bf16[1,1536,1536]{2,1,0:T(8,128)(2,1)} async-done(((bf16[1,1536,384]{2,1,0:T(8,128)(2,1)}), bf16[1,1536,1536]{2,1,0:T(8,128)(2,1)}) %all-gather.11.cloned.1.call-update) | async-done | bytes 4718608 | tf_op jit(solution)/shard_map/all_gather | solution.py:100
  104.4 10.2 pmax.14
  117.4 10.3 psum.84
  138.4 22.2 %reduce-scatter.37.cloned.1.call-done = bf16[384,128]{1,0:T(8,128)(2,1)} async-done(((bf16[1536,128]{1,0:T(8,128)(2,1)}), bf16[384,128]{1,0:T(8,128)(2,1)}) %reduce-scatter.37.cloned.1.call-update) | async-done | bytes 98320
  163.0 33.0 %all-reduce.13.cloned.1.call-done = bf16[2,64,1536]{2,1,0:T(8,128)(2,1)} async-done(((bf16[2,64,1536]{2,1,0:T(8,128)(2,1)}), bf16[2,64,1536]{2,1,0:T(8,128)(2,1)}) %all-reduce.13.cloned.1.call-update) | async-done | bytes 393232 | tf_op jit(solution)/shard_map/psum | solution.py:35
  208.2 31.4 %all-reduce.15.cloned.1.call-done = bf16[2,64,1536]{2,1,0:T(8,128)(2,1)} async-done(((bf16[2,64,1536]{2,1,0:T(8,128)(2,1)}), bf16[2,64,1536]{2,1,0:T(8,128)(2,1)}) %all-reduce.15.cloned.1.call-update) | async-done | bytes 393232 | tf_op jit(solution)/shard_map/psum | solution.py:35
  242.0 36.5 %all-gather.13.cloned.1.call-done = bf16[1,1536,1536]{2,1,0:T(8,128)(2,1)} async-done(((bf16[1,1536,384]{2,1,0:T(8,128)(2,1)}), bf16[1,1536,1536]{2,1,0:T(8,128)(2,1)}) %all-gather.13.cloned.1.call-update) | async-done | bytes 4718608 | tf_op jit(solution)/shard_map/all_gather | solution.py:101
  291.0 26.4 %all-gather.15.cloned.1.call-done = bf16[1,1536,1536]{2,1,0:T(8,128)(2,1)} async-done(((bf16[1,1536,384]{2,1,0:T(8,128)(2,1)}), bf16[1,1536,1536]{2,1,0:T(8,128)(2,1)}) %all-gather.15.cloned.1.call-update) | async-done | bytes 4718608 | tf_op jit(solution)/shard_map/all_gather | solution.py:100
  339.9 10.4 pmax.15
  353.1 10.1 psum.87
  369.8 21.8 %reduce-scatter.39.cloned.1.call-done = bf16[384,128]{1,0:T(8,128)(2,1)} async-done(((bf16[1536,128]{1,0:T(8,128)(2,1)}), bf16[384,128]{1,0:T(8,128)(2,1)}) %reduce-scatter.39.cloned.1.call-update) | async-done | bytes 98320
  395.3 32.7 %all-reduce.17.cloned.1.call-done = bf16[2,64,1536]{2,1,0:T(8,128)(2,1)} async-done(((bf16[2,64,1536]{2,1,0:T(8,128)(2,1)}), bf16[2,64,1536]{2,1,0:T(8,128)(2,1)}) %all-reduce.17.cloned.1.call-update) | async-done | bytes 393232 | tf_op jit(solution)/shard_map/psum | solution.py:35
  442.7 32.7 %all-reduce.19.cloned.1.call-done = bf16[2,64,1536]{2,1,0:T(8,128)(2,1)} async-done(((bf16[2,64,1536]{2,1,0:T(8,128)(2,1)}), bf16[2,64,1536]{2,1,0:T(8,128)(2,1)}) %all-reduce.19.cloned.1.call-update) | async-done | bytes 393232 | tf_op jit(solution)/shard_map/psum | solution.py:39
  493.2 10.8 psum.91
  552.1 33.3 %all-reduce.21.cloned.1.call-done = bf16[2,64,1536]{2,1,0:T(8,128)(2,1)} async-done(((bf16[2,64,1536]{2,1,0:T(8,128)(2,1)}), bf16[2,64,1536]{2,1,0:T(8,128)(2,1)}) %all-reduce.21.cloned.1.call-update) | async-done | bytes 393232 | tf_op jit(solution)/shard_map/psum | solution.py:39
  606.7 25.2 %all-reduce.23.cloned.1.call-done = bf16[2,64,1536]{2,1,0:T(8,128)(2,1)} async-done(((bf16[2,64,1536]{2,1,0:T(8,128)(2,1)}), bf16[2,64,1536]{2,1,0:T(8,128)(2,1)}) %all-reduce.23.cloned.1.call-update) | async-done | bytes 393232 | tf_op jit(solution)/shard_map/psum | solution.py:39
  652.2 10.8 psum.94
  718.2 25.4 %all-reduce.27.cloned.1.call-done = (bf16[2,64,1536]{2,1,0:T(8,128)(2,1)}, bf16[2,64,1536]{2,1,0:T(8,128)(2,1)}) async-done(((bf16[2,64,1536]{2,1,0:T(8,128)(2,1)}, bf16[2,64,1536]{2,1,0:T(8,128)(2,1)}), (bf16[2,64,1536]{2,1,0:T(8,128)(2,1)}, bf16[2,64,1536]{2,1,0:T(8,128)(2,1)})) %all-reduce.27.cloned.1.call-update) | async-done | bytes 786448 | tf_op jit(solution)/shard_map/psum | solution.py:35
  761.0 8.3 pad_maximum_fusion.3
  769.4 24.1 %copy.160 = bf16[2,1536,1536]{1,0,2:T(2,128)(2,1)} copy(bf16[2,1536,1536]{2,1,0:T(8,128)(2,1)} %pad_maximum_fusion.3) | data formatting | bytes 18874368 | tf_op jit(solution)/shard_map/stack | solution.py:309
  812.0 8.3 pad_maximum_fusion.2
  863.0 7.1 pad_maximum_fusion.1
  873.4 34.3 %reduce-scatter.47.cloned.1.call-done = f32[48,2]{1,0:T(8,128)} async-done(((f32[1536,2]{1,0:T(8,128)}), f32[48,2]{1,0:T(8,128)}) %reduce-scatter.47.cloned.1.call-update) | async-done | bytes 400
  909.2 98.1 %reduce-scatter.45.cloned.1.call-done = f32[48,4]{1,0:T(8,128)} async-done(((f32[1536,4]{1,0:T(8,128)}), f32[48,4]{1,0:T(8,128)}) %reduce-scatter.45.cloned.1.call-update) | async-done | bytes 784
  1011.0 60.7 %reduce-scatter.49.cloned.1.call-done = bf16[192,2]{1,0:T(8,128)(2,1)} async-done(((bf16[1536,2]{1,0:T(8,128)(2,1)}), bf16[192,2]{1,0:T(8,128)(2,1)}) %reduce-scatter.49.cloned.1.call-update) | async-done | bytes 784
  1073.1 70.6 %reduce-scatter.29.cloned.1.call-done = bf16[2,192,384]{2,1,0:T(8,128)(2,1)} async-done(((bf16[2,1536,384]{2,1,0:T(8,128)(2,1)}), bf16[2,192,384]{2,1,0:T(8,128)(2,1)}) %reduce-scatter.29.cloned.1.call-update) | async-done | bytes 294928 | tf_op jit(solution)/shard_map/reduce_scatter | solution.py:296
  1145.6 364.5 %all-reduce.25.cloned.1.call-done = (bf16[2,384,1536]{1,0,2:T(2,128)(2,1)}, bf16[2,1536,1536]{1,0,2:T(2,128)(2,1)}) async-done(((bf16[2,384,1536]{1,0,2:T(2,128)(2,1)}, bf16[2,1536,1536]{1,0,2:T(2,128)(2,1)}), (bf16[2,384,1536]{1,0,2:T(2,128)(2,1)}, bf16[2,1536,1536]{1,0,2:T(2,128)(2,1)})) %all-reduce.25.cloned.1.call-update) | async-done | bytes 11796496
  1516.0 160.5 %reduce-scatter.35.cloned.1.call-done = bf16[2,192,1536]{2,1,0:T(8,128)(2,1)} async-done(((bf16[2,1536,1536]{2,1,0:T(8,128)(2,1)}), bf16[2,192,1536]{2,1,0:T(8,128)(2,1)}) %reduce-scatter.35.cloned.1.call-update) | async-done | bytes 1179664 | tf_op jit(solution)/shard_map/reduce_scatter | solution.py:305
  1679.4 209.3 %reduce-scatter.31.cloned.1.call-done = f32[2,192,384]{2,1,0:T(8,128)} async-done(((f32[2,6144,384]{2,1,0:T(8,128)}), f32[2,192,384]{2,1,0:T(8,128)}) %reduce-scatter.31.cloned.1.call-update) | async-done | bytes 589840 | tf_op jit(solution)/shard_map/reduce_scatter | solution.py:278
  1888.7 211.9 %reduce-scatter.33.cloned.1.call-done = f32[2,192,384]{2,1,0:T(8,128)} async-done(((f32[2,6144,384]{2,1,0:T(8,128)}), f32[2,192,384]{2,1,0:T(8,128)}) %reduce-scatter.33.cloned.1.call-update) | async-done | bytes 589840 | tf_op jit(solution)/shard_map/reduce_scatter | solution.py:284
  (424 shorter events, 391.8 us)
Async XLA Ops:
  7.2 43.7 %all-gather.9.cloned.1.call-start = ((), (), s32[]{:S(2)}) async-start(), calls=%async_computation.22 | async-start | bytes 5898240 | tf_op jit(solution)/shard_map/all_gather | solution.py:101
  10.7 79.8 %all-gather.11.cloned.1.call-start = ((), (), s32[]{:S(2)}) async-start(), calls=%async_computation.23 | async-start | bytes 5898240 | tf_op jit(solution)/shard_map/all_gather | solution.py:100
  12.5 148.1 %reduce-scatter.37.cloned.1.call-start = ((), (), s32[]{:S(2)}) async-start(), calls=%async_computation.26 | async-start | bytes 491520
  26.1 64.4 %copy-start.49 = (bf16[2,16,1536]{2,1,0:T(8,128)(2,1)}, bf16[2,16,1536]{2,1,0:T(8,128)(2,1)S(1)}, u32[]{:S(2)}) copy-start(bf16[2,16,1536]{2,1,0:T(8,128)(2,1)S(1)} %constant_dynamic-slice_fusion.1) | copy-start | bytes 294916
  138.3 57.7 %all-reduce.13.cloned.1.call-start = ((), (), s32[]{:S(2)}) async-start(), calls=%async_computation.12 | async-start | bytes 786432 | tf_op jit(solution)/shard_map/psum | solution.py:35
  162.9 76.7 %all-reduce.15.cloned.1.call-start = ((), (), s32[]{:S(2)}) async-start(), calls=%async_computation.13 | async-start | bytes 786432 | tf_op jit(solution)/shard_map/psum | solution.py:35
  197.2 434.8 %copy-start.8 = (f32[2,64,1536]{2,1,0:T(8,128)}, f32[2,64,1536]{2,1,0:T(8,128)S(1)}, u32[]{:S(2)}) copy-start(f32[2,64,1536]{2,1,0:T(8,128)S(1)} %get-tuple-element.107) | copy-start | bytes 2359300
  206.8 71.6 %all-gather.13.cloned.1.call-start = ((), (), s32[]{:S(2)}) async-start(), calls=%async_computation.24 | async-start | bytes 5898240 | tf_op jit(solution)/shard_map/all_gather | solution.py:101
  206.8 71.6 %copy-start.24 = (bf16[2,256,1536]{2,1,0:T(8,128)(2,1)S(1)}, bf16[2,256,1536]{2,1,0:T(8,128)(2,1)}, u32[]{:S(2)}) copy-start(bf16[2,256,1536]{2,1,0:T(8,128)(2,1)} %get-tuple-element.112) | copy-start | bytes 4718596
  207.4 110.0 %all-gather.15.cloned.1.call-start = ((), (), s32[]{:S(2)}) async-start(), calls=%async_computation.25 | async-start | bytes 5898240 | tf_op jit(solution)/shard_map/all_gather | solution.py:100
  208.1 183.5 %reduce-scatter.39.cloned.1.call-start = ((), (), s32[]{:S(2)}) async-start(), calls=%async_computation.27 | async-start | bytes 491520
  242.0 75.5 %copy-start.51 = (bf16[2,16,1536]{2,1,0:T(8,128)(2,1)}, bf16[2,16,1536]{2,1,0:T(8,128)(2,1)S(1)}, u32[]{:S(2)}) copy-start(bf16[2,16,1536]{2,1,0:T(8,128)(2,1)S(1)} %constant_dynamic-slice_fusion) | copy-start | bytes 294916
  369.6 58.4 %all-reduce.17.cloned.1.call-start = ((), (), s32[]{:S(2)}) async-start(), calls=%async_computation.14 | async-start | bytes 786432 | tf_op jit(solution)/shard_map/psum | solution.py:35
  395.2 80.3 %all-reduce.19.cloned.1.call-start = ((), (), s32[]{:S(2)}) async-start(), calls=%async_computation.15 | async-start | bytes 786432 | tf_op jit(solution)/shard_map/psum | solution.py:39
  442.7 104.6 %reduce-scatter.41.cloned.1.call-start = ((), (), s32[]{:S(2)}) async-start(), calls=%async_computation.28 | async-start | bytes 491520
  478.7 108.1 %copy-start.16 = (f32[2,64,1536]{2,1,0:T(8,128)}, f32[2,64,1536]{2,1,0:T(8,128)S(1)}, u32[]{:S(2)}) copy-start(f32[2,64,1536]{2,1,0:T(8,128)S(1)} %fusion.215) | copy-start | bytes 2359300
  518.2 67.2 %all-reduce.21.cloned.1.call-start = ((), (), s32[]{:S(2)}) async-start(), calls=%async_computation.16 | async-start | bytes 786432 | tf_op jit(solution)/shard_map/psum | solution.py:39
  552.0 79.9 %all-reduce.23.cloned.1.call-start = ((), (), s32[]{:S(2)}) async-start(), calls=%async_computation.17 | async-start | bytes 786432 | tf_op jit(solution)/shard_map/psum | solution.py:39
  599.2 104.1 %reduce-scatter.43.cloned.1.call-start = ((), (), s32[]{:S(2)}) async-start(), calls=%async_computation.29 | async-start | bytes 491520
  676.5 67.0 %all-reduce.27.cloned.1.call-start = ((), (), s32[]{:S(2)}) async-start(), calls=%async_computation.35 | async-start | bytes 1572864 | tf_op jit(solution)/shard_map/psum | solution.py:35
  708.0 163.9 %reduce-scatter.51.cloned.1.call-start = ((), (), s32[]{:S(2)}) async-start(), calls=%async_computation.33 | async-start | bytes 442368
  708.6 199.2 %reduce-scatter.47.cloned.1.call-start = ((), (), s32[]{:S(2)}) async-start(), calls=%async_computation.31 | async-start | bytes 811008
  709.9 297.4 %reduce-scatter.45.cloned.1.call-start = ((), (), s32[]{:S(2)}) async-start(), calls=%async_computation.30 | async-start | bytes 811008
  716.7 355.0 %reduce-scatter.49.cloned.1.call-start = ((), (), s32[]{:S(2)}) async-start(), calls=%async_computation.32 | async-start | bytes 442368
  746.0 397.8 %reduce-scatter.29.cloned.1.call-start = ((), (), s32[]{:S(2)}) async-start(), calls=%async_computation.18 | async-start | bytes 2654208 | tf_op jit(solution)/shard_map/reduce_scatter | solution.py:296
  747.8 762.3 %all-reduce.25.cloned.1.call-start = ((), (), s32[]{:S(2)}) async-start(), calls=%async_computation.34 | async-start | bytes 23592960
  802.5 874.0 %reduce-scatter.35.cloned.1.call-start = ((), (), s32[]{:S(2)}) async-start(), calls=%async_computation.21 | async-start | bytes 10616832 | tf_op jit(solution)/shard_map/reduce_scatter | solution.py:305
  820.3 1068.5 %reduce-scatter.31.cloned.1.call-start = ((), (), s32[]{:S(2)}) async-start(), calls=%async_computation.19 | async-start | bytes 19464192 | tf_op jit(solution)/shard_map/reduce_scatter | solution.py:278
  852.5 1248.2 %reduce-scatter.33.cloned.1.call-start = ((), (), s32[]{:S(2)}) async-start(), calls=%async_computation.20 | async-start | bytes 19464192 | tf_op jit(solution)/shard_map/reduce_scatter | solution.py:284
  870.0 138.6 %copy-start.53 = (bf16[2,64,1536]{2,1,0:T(8,128)(2,1)S(1)}, bf16[2,64,1536]{2,1,0:T(8,128)(2,1)}, u32[]{:S(2)}) copy-start(bf16[2,64,1536]{2,1,0:T(8,128)(2,1)} %get-tuple-element.98) | copy-start | bytes 1179652
  870.1 139.7 %copy-start.43 = (bf16[2,64,1536]{2,1,0:T(8,128)(2,1)S(1)}, bf16[2,64,1536]{2,1,0:T(8,128)(2,1)}, u32[]{:S(2)}) copy-start(bf16[2,64,1536]{2,1,0:T(8,128)(2,1)} %get-tuple-element.99) | copy-start | bytes 1179652
  1512.1 588.6 %copy-start.1 = (f32[4,1536]{1,0:T(4,128)S(1)}, f32[4,1536]{1,0:T(4,128)}, u32[]{:S(2)}) copy-start(f32[4,1536]{1,0:T(4,128)} %param.19) | copy-start | bytes 73732
  (87 other events, 835.9 us)
Sparse Core Ops, SparseCore 0:
  10.8 40.0 all-gather.8
  53.1 37.3 all-gather.10
  138.4 22.0 reduce-scatter.36
  163.4 32.5 all-reduce.12
  206.9 32.6 all-reduce.14
  241.0 37.3 all-gather.12
  280.0 37.3 all-gather.14
  369.7 21.8 reduce-scatter.38
  395.3 32.5 all-reduce.16
  442.8 32.6 all-reduce.18
  518.3 21.4 reduce-scatter.40
  552.1 33.2 all-reduce.20
  599.3 32.6 all-reduce.22
  676.7 21.4 reduce-scatter.42
  708.1 35.3 all-reduce.26
  746.7 61.5 reduce-scatter.50
  813.2 94.5 reduce-scatter.46
  912.8 94.4 reduce-scatter.44
  1011.1 60.4 reduce-scatter.48
  1075.5 68.1 reduce-scatter.28
  1147.9 362.1 all-reduce.24
  1514.1 162.3 reduce-scatter.34
  1684.6 204.0 reduce-scatter.30
  1896.7 203.8 reduce-scatter.32
where the time goes:
time: 2120 us; the launch traced here: 2110 us
  waiting for transfers between devices  1580 us (75%)
  matrix products  189 us (9%)
  local copies, waits for them, and re-layouts  134 us (6%)
  other arithmetic  92.5 us (4%)
  blocking collectives  90.4 us (4%)
    unnamed x33, waiting for transfers between devices  604 us
    reduce_scatter x1, waiting for transfers between devices, on_device(): lax.psum_scatter(block_layout(value_stack, clip_total, frame_count), ('cl...  212 us
    reduce_scatter x1, waiting for transfers between devices, on_device(): lax.psum_scatter(block_layout(key_stack, clip_total, frame_count), ('clip...  209 us
    reduce_scatter x1, waiting for transfers between devices, on_device(): lax.psum_scatter(jnp.stack(up_grads[::-1]).astype(jnp.bfloat16), 'clip',...  160 us
    psum x4, waiting for transfers between devices, latent_sums(): lax.psum(partial_sum.astype(jnp.bfloat16), 'frame').astype(jnp.float32)  122 us
    psum x3, waiting for transfers between devices, latent_grads(): lax.psum(partial_sum.astype(jnp.bfloat16), 'frame').astype(jnp.float32)  91.3 us
    reduce_scatter x1, waiting for transfers between devices, on_device(): lax.psum_scatter(jnp.stack(query_grads[::-1]).astype(jnp.bfloat16), 'clip...  70.6 us
    all_gather x2, waiting for transfers between devices, on_device(): lax.all_gather(value_weight[layer_no], 'frame', axis=1, tiled=True)  58.8 us
  transfers between devices with their start and end apart: 24, of which 21 were waited for; matrix products, arithmetic and copies ran while one was open for 12% of the time, Pallas kernels for 0%

commit v1 on v0

v1 whole, which is shorter than its diff:
```python
import jax
import jax.numpy as jnp
from jax import lax
from jax.sharding import PartitionSpec as P

HEAD_DIM = 96
SLOTS = 4
LAYERS = 2
EPSILON = 1e-05
SCALING = HEAD_DIM ** (-0.5)
f32 = jnp.float32
bf16 = jnp.bfloat16


def norm_plain(v):
    mean = jnp.mean(v, axis=-1, keepdims=True)
    centred = v - mean
    inverse = lax.rsqrt(jnp.mean(centred * centred, axis=-1, keepdims=True) + EPSILON)
    return centred * inverse, inverse


def norm_back(u, normed, inverse):
    return inverse * (
        u
        - jnp.mean(u, axis=-1, keepdims=True)
        - normed * jnp.mean(u * normed, axis=-1, keepdims=True)
    )


def dot(a, b):
    return jnp.dot(a, b, preferred_element_type=f32)


def dot_nt(a, b):
    return lax.dot_general(a, b, (((1,), (1,)), ((), ())), preferred_element_type=f32)


def dot_tn(a, b):
    return lax.dot_general(a, b, (((0,), (0,)), ((), ())), preferred_element_type=f32)


def swap(v, axis, bit):
    size = lax.axis_size(axis)
    return lax.ppermute(v, axis, [(i, i ^ bit) for i in range(size)])


def bits_of(size):
    out, bit = [], 1
    while bit < size:
        out.append(bit)
        bit *= 2
    return out


def frame_sum(part, core):
    keep = lax.dynamic_index_in_dim(part, core, 0, keepdims=False)
    send = lax.dynamic_index_in_dim(part, 1 - core, 0, keepdims=False).astype(bf16)
    total = keep.astype(bf16).astype(f32) + swap(send, "frame", 1).astype(f32)
    for bit in bits_of(lax.axis_size("frame"))[1:]:
        mine = total.astype(bf16)
        total = mine.astype(f32) + swap(mine, "frame", bit).astype(f32)
    mine = total.astype(bf16)
    other = swap(mine, "frame", 1)
    first = jnp.where(core == 0, mine, other)
    second = jnp.where(core == 0, other, mine)
    return jnp.concatenate([first, second], axis=0).astype(f32)


def gather_rows(rows, frame_here):
    count = rows.shape[0] // lax.axis_size("frame")
    have = lax.dynamic_slice_in_dim(rows, frame_here * count, count, 0)
    for bit in bits_of(lax.axis_size("clip")):
        have = jnp.concatenate([have, swap(have, "clip", bit)], axis=0)
    for bit in bits_of(lax.axis_size("frame"))[::-1]:
        have = jnp.concatenate([have, swap(have, "frame", bit)], axis=0)
    return have


def scatter_rows(part, clip_here):
    total = part
    for bit in bits_of(lax.axis_size("clip")):
        mine = (clip_here // bit) % 2
        rows, width = total.shape
        blocks = lax.axis_size("clip") // bit
        halves = total.reshape(blocks // 2, 2, rows // blocks, width)
        keep = lax.dynamic_index_in_dim(halves, mine, 1, keepdims=False)
        send = lax.dynamic_index_in_dim(halves, 1 - mine, 1, keepdims=False).astype(bf16)
        total = keep.astype(f32) + swap(send, "clip", bit).astype(f32)
        total = total.reshape(rows // 2, width)
    return total


def gelu_parts(x):
    half = 0.5 * (1.0 + lax.erf(x * (0.5**0.5)))
    return x * half, half + x * jnp.exp(-0.5 * x * x) * (0.5 / jnp.pi) ** 0.5


def on_device(
    media, frame_order, clip_counts, latents, time_embed, media_gain, latent_gain, ffn_gain,
    query_weight, key_weight, value_weight, out_weight, up_weight, down_weight, cotangent,
):
    clips, _, patches, width = media.shape
    lat_rows = latents.shape[1]
    nf = lax.axis_size("frame")
    nc = lax.axis_size("clip")
    frame_here = lax.axis_index("frame")
    clip_here = lax.axis_index("clip")
    core = frame_here % 2
    own = query_weight.shape[2]
    heads = own // HEAD_DIM
    rows = clips * lat_rows

    clip_ids = clip_here * clips + jnp.arange(clips, dtype=jnp.int32)
    owner_match = (clip_ids // SLOTS)[:, None] == jnp.arange(clip_counts.shape[0], dtype=jnp.int32)[None, :]
    owner_count = jnp.sum(jnp.where(owner_match, clip_counts[None, :], 0), axis=1)
    living = (clip_ids % SLOTS < owner_count).astype(f32)
    living = jnp.repeat(living, lat_rows)[:, None]

    frames = [media[:, 0]]
    for bit in bits_of(nf)[::-1]:
        got = [swap(m, "frame", bit) for m in frames]
        frames = frames + got
    rel = [0]
    for bit in bits_of(nf)[::-1]:
        rel = rel + [r ^ bit for r in rel]
    frames = [frames[rel.index(r)] for r in range(nf)]

    times = jnp.arange(nf, dtype=jnp.int32)
    plain_b, plain0, inv0, onehot0 = [], None, None, None
    for r in range(nf):
        order = lax.dynamic_index_in_dim(frame_order, frame_here ^ r, 1, keepdims=False)
        onehot = (order[:, None] == times[None, :]).astype(f32)
        stamp = jnp.dot(onehot, time_embed, precision=lax.Precision.HIGHEST)
        plain, inv = norm_plain(frames[r].astype(f32) + stamp[:, None, :])
        if r == 0:
            plain0, inv0, onehot0 = plain, inv, onehot
        plain_b.append(plain.astype(bf16).reshape(clips * patches, width))

    wide = jnp.concatenate(
        [
            (media_gain[l][:, None] * w[l].astype(f32)).astype(bf16)
            for l in range(LAYERS)
            for w in (key_weight, value_weight)
        ],
        axis=1,
    )
    kv_media = [dot(p, wide).astype(bf16).reshape(clips, patches, -1) for p in plain_b]

    head_of = jnp.arange(own, dtype=jnp.int32) // HEAD_DIM
    mask = (head_of[None, :] == jnp.arange(heads, dtype=jnp.int32)[:, None]).astype(bf16)

    def spread(v):
        return (v[:, None] * mask[None, :, None, :]).reshape(clips, heads * lat_rows, own)

    def gathered(v):
        v = v.reshape(clips, heads, lat_rows, own) * mask[None, :, None, :].astype(f32)
        return jnp.sum(v, axis=1)

    stored = []
    current = latents.reshape(rows, width)
    for l in range(LAYERS):
        lat_plain, lat_inv = norm_plain(current)
        lat_n = (lat_plain * latent_gain[l]).astype(bf16)
        q = dot(lat_n, query_weight[l]).astype(bf16)
        kl = dot(lat_n, key_weight[l]).astype(bf16).reshape(clips, lat_rows, own)
        vl = dot(lat_n, value_weight[l]).astype(bf16).reshape(clips, lat_rows, own)
        keys = jnp.concatenate([kv[:, :, 2 * l * own : (2 * l + 1) * own] for kv in kv_media] + [kl], axis=1)
        values = jnp.concatenate([kv[:, :, (2 * l + 1) * own : (2 * l + 2) * own] for kv in kv_media] + [vl], axis=1)
        qs = spread(q.reshape(clips, lat_rows, own))
        scores = jnp.einsum("cqd,ckd->cqk", qs, keys, preferred_element_type=f32) * SCALING
        top = jnp.max(scores, axis=-1, keepdims=True)
        ex = jnp.exp(scores - top)
        soft = (ex / jnp.sum(ex, axis=-1, keepdims=True)).astype(bf16)
        att = gathered(jnp.einsum("cqk,ckd->cqd", soft, values, preferred_element_type=f32))
        att = att.reshape(rows, own).astype(bf16)
        middle = current + frame_sum(dot(att, out_weight[l]).reshape(2, rows // 2, width), core)
        ffn_plain, ffn_inv = norm_plain(middle)
        ffn_in = (ffn_plain * ffn_gain[l]).astype(bf16)
        hidden, slope = gelu_parts(dot(ffn_in, up_weight[l]))
        current = middle + frame_sum(
            dot(hidden.astype(bf16), down_weight[l]).reshape(2, rows // 2, width), core
        )
        stored.append((lat_plain, lat_inv, lat_n, qs, keys, values, soft, att, ffn_plain, ffn_inv, ffn_in, slope))
    latents_out = current * living

    grad = cotangent.reshape(rows, width) * living
    proj_grads, up_grads, down_grads = [None] * LAYERS, [None] * LAYERS, [None] * LAYERS
    lat_gain_grads, ffn_gain_grads, media_gain_grads = [None] * LAYERS, [None] * LAYERS, [None] * LAYERS
    gkv = [None] * LAYERS
    for l in reversed(range(LAYERS)):
        lat_plain, lat_inv, lat_n, qs, keys, values, soft, att, ffn_plain, ffn_inv, ffn_in, slope = stored[l]
        gy = grad.astype(bf16)
        gpre = (slope * dot_nt(gy, down_weight[l])).astype(bf16)
        gffn = frame_sum(dot_nt(gpre, up_weight[l]).reshape(2, rows // 2, width), core)
        ffn_gain_grads[l] = jnp.sum(gffn * ffn_plain, axis=0)
        gmid = grad + norm_back(gffn * ffn_gain[l], ffn_plain, ffn_inv)
        gupd = gmid.astype(bf16)
        gatt = dot_nt(gupd, out_weight[l]).astype(bf16).reshape(clips, lat_rows, own)
        gatts = spread(gatt)
        gsoft = jnp.einsum("cqd,ckd->cqk", gatts, values, preferred_element_type=f32)
        soft32 = soft.astype(f32)
        delta = jnp.sum(soft32 * gsoft, axis=-1, keepdims=True)
        gscore = (soft32 * (gsoft - delta)).astype(bf16)
        gq = (gathered(jnp.einsum("cqk,ckd->cqd", gscore, keys, preferred_element_type=f32)) * SCALING).astype(bf16).reshape(rows, own)
        gk = (jnp.einsum("cqk,cqd->ckd", gscore, qs, preferred_element_type=f32) * SCALING).astype(bf16)
        gv = jnp.einsum("cqk,cqd->ckd", soft, gatts, preferred_element_type=f32).astype(bf16)
        gkl = gk[:, nf * patches :].reshape(rows, own)
        gvl = gv[:, nf * patches :].reshape(rows, own)
        glat = frame_sum(
            (dot_nt(gq, query_weight[l]) + dot_nt(gkl, key_weight[l]) + dot_nt(gvl, value_weight[l])).reshape(2, rows // 2, width), core
        )
        lat_gain_grads[l] = jnp.sum(glat * lat_plain, axis=0)
        grad = gmid + norm_back(glat * latent_gain[l], lat_plain, lat_inv)

        fa = gather_rows(ffn_in, frame_here)
        ga = gather_rows(gy, frame_here)
        hid_a, slope_a = gelu_parts(dot(fa, up_weight[l]))
        gpre_a = (slope_a * dot_nt(ga, down_weight[l])).astype(bf16)
        cols = width // nc
        fs = lax.dynamic_slice_in_dim(fa, clip_here * cols, cols, 1)
        gs = lax.dynamic_slice_in_dim(ga, clip_here * cols, cols, 1)
        up_grads[l] = dot_tn(fs, gpre_a)
        down_grads[l] = dot_tn(hid_a.astype(bf16), gs)

        gkm = [gk[:, r * patches : (r + 1) * patches].reshape(clips * patches, own) for r in range(nf)]
        gvm = [gv[:, r * patches : (r + 1) * patches].reshape(clips * patches, own) for r in range(nf)]
        kraw = sum(dot_tn(plain_b[r], gkm[r]) for r in range(nf))
        vraw = sum(dot_tn(plain_b[r], gvm[r]) for r in range(nf))
        media_gain_grads[l] = jnp.sum(kraw * key_weight[l].astype(f32) + vraw * value_weight[l].astype(f32), axis=1)
        kg = kraw * media_gain[l][:, None] + dot_tn(lat_n, gkl)
        vg = vraw * media_gain[l][:, None] + dot_tn(lat_n, gvl)
        qg = dot_tn(lat_n, gq)
        og = dot_tn(gupd, att)
        proj_grads[l] = scatter_rows(jnp.concatenate([qg, kg, vg, og], axis=1), clip_here)
        gkv[l] = (gkm, gvm)

    u = [
        dot_nt(jnp.concatenate([g for l in range(LAYERS) for g in (gkv[l][0][r], gkv[l][1][r])], axis=1), wide)
        for r in range(nf)
    ]
    for bit in bits_of(nf):
        step = [r for r in range(nf) if u[r] is not None and r & bit]
        for r in step:
            u[r ^ bit] = u[r ^ bit] + swap(u[r].astype(bf16), "frame", bit).astype(f32)
            u[r] = None
    media_grad = norm_back(u[0].reshape(clips, patches, width), plain0, inv0)
    time_part = jnp.dot(onehot0.T, jnp.sum(media_grad, axis=1), precision=lax.Precision.HIGHEST)

    n_all = nc * nf
    narrow = jnp.concatenate([time_part, jnp.stack(media_gain_grads)], axis=0)
    narrow = narrow.reshape(nf + 2, n_all, width // n_all).transpose(1, 0, 2).reshape(n_all, -1)
    broad = jnp.concatenate([jnp.stack(lat_gain_grads), jnp.stack(ffn_gain_grads)], axis=0)
    broad = broad.reshape(4, nc, width // nc).transpose(1, 0, 2).reshape(nc, 1, -1)
    broad = broad * (jnp.arange(nf) == frame_here).astype(f32)[None, :, None]
    packed = jnp.concatenate([narrow, broad.reshape(n_all, -1)], axis=1)
    packed = jnp.sum(lax.all_to_all(packed, ("clip", "frame"), 0, 0, tiled=True), axis=0)
    cut = (nf + 2) * (width // n_all)
    narrow = packed[:cut].reshape(nf + 2, -1)
    broad = packed[cut:].reshape(4, -1)

    proj = jnp.stack(proj_grads)
    return (
        latents_out.reshape(latents.shape),
        media_grad[:, None],
        grad.reshape(latents.shape),
        narrow[:nf],
        narrow[nf:],
        broad[:2],
        broad[2:],
        proj[:, :, :own],
        proj[:, :, own : 2 * own],
        proj[:, :, 2 * own : 3 * own],
        jnp.swapaxes(proj[:, :, 3 * own :], 1, 2),
        jnp.stack(up_grads),
        jnp.stack(down_grads),
    )


def solution(mesh):
    return jax.shard_map(
        on_device,
        mesh=mesh,
        in_specs=(
            P("clip", "frame", None, None),
            P("clip", None),
            P(),
            P("clip", None, None),
            P(),
            P(),
            P(),
            P(),
            P(None, None, "frame"),
            P(None, None, "frame"),
            P(None, None, "frame"),
            P(None, "frame", None),
            P(None, None, "frame"),
            P(None, "frame", None),
            P("clip", None, None),
        ),
        out_specs=(
            P("clip", None, None),
            P("clip", "frame", None, None),
            P("clip", None, None),
            P(None, ("clip", "frame")),
            P(None, ("clip", "frame")),
            P(None, "clip"),
            P(None, "clip"),
            P(None, "clip", "frame"),
            P(None, "clip", "frame"),
            P(None, "clip", "frame"),
            P(None, "frame", "clip"),
            P(None, "clip", "frame"),
            P(None, "frame", "clip"),
        ),
        check_vma=False,
    )
```

time: 2120 us -> 673 us (0.32)
  waiting for transfers between devices: 1580 us -> 134 us
  blocking collectives: 90.4 us -> 0 us
  starting transfers between devices: 2.42 us -> 45.3 us
  other arithmetic: 92.5 us -> 129 us
  matrix products: 189 us -> 215 us
    reduce_scatter x4 -> x0, waiting for transfers between devices: 652 us -> none  [the longest x1 212 us: on_device(): lax.psum_scatter(block_layout(value_stack, clip_total, frame_count), ('cl...]
    unnamed x33 -> x0, waiting for transfers between devices: 604 us -> none
    psum x7 -> x0, waiting for transfers between devices: 214 us -> none  [the longest x4 122 us: latent_sums(): lax.psum(partial_sum.astype(jnp.bfloat16), 'frame').astype(jnp.float32)]
    ppermute x0 -> x56, waiting for transfers between devices: none -> 134 us  [swap(): return lax.ppermute(v, axis, [(i, i ^ bit) for i in range(size)])]
    all_gather x4 -> x0, waiting for transfers between devices: 113 us -> none  [the longest x2 58.8 us: on_device(): lax.all_gather(value_weight[layer_no], 'frame', axis=1, tiled=True)]
    psum x4 -> x0, blocking collectives: 41.9 us -> none  [the longest x2 21.5 us: on_device(): delta_sum = lax.psum(local_delta, 'frame')]
    ppermute x0 -> x56, starting transfers between devices: none -> 41.7 us  [swap(): return lax.ppermute(v, axis, [(i, i ^ bit) for i in range(size)])]
    another operation x10 -> x0, local copies, waits for them, and re-layouts: 39.8 us -> none  [the longest x1 24.1 us: on_device(): jnp.stack(down_grads[::-1]).astype(jnp.bfloat16)]
  transfers between devices with their start and end apart: 24 -> 57, of which waited for: 21 -> 21; matrix products, arithmetic and copies ran while one was open for 12% -> 59% of each run, Pallas kernels for 0% -> 0%
where the time goes in v1:
time: 673 us; the launch traced here: 668 us
  matrix products  215 us (32%)
  local copies, waits for them, and re-layouts  140 us (21%)
  waiting for transfers between devices  134 us (20%)
  other arithmetic  129 us (19%)
  starting transfers between devices  45.3 us (7%)
    ppermute x56, waiting for transfers between devices, swap(): return lax.ppermute(v, axis, [(i, i ^ bit) for i in range(size)])  134 us
    dot_general x28, matrix products, dot_tn(): lax.dot_general(a, b, (((0,), (0,)), ((), ())), preferred_element_type=f32)  83.8 us
    unnamed x430, local copies, waits for them, and re-layouts  66.2 us
    dot_general x18, matrix products, dot(): return jnp.dot(a, b, preferred_element_type=f32)  59.8 us
    dot_general x16, matrix products, dot_nt(): lax.dot_general(a, b, (((1,), (1,)), ((), ())), preferred_element_type=f32)  42 us
    ppermute x56, starting transfers between devices, swap(): return lax.ppermute(v, axis, [(i, i ^ bit) for i in range(size)])  41.7 us
    concatenate x2, local copies, waits for them, and re-layouts, on_device(): jnp.concatenate([qg, kg, vg, og], axis=1)  19.5 us
    concatenate x12, other arithmetic, gather_rows(): have = jnp.concatenate([have, swap(have, 'clip', bit)], axis=0)  16.7 us
  transfers between devices with their start and end apart: 57, of which 21 were waited for; matrix products, arithmetic and copies ran while one was open for 59% of the time, Pallas kernels for 0%

profile of v1, /device:TPU:0, one launch (start us, length us, event | category | flops | bytes accessed | tf_op | source)
XLA Modules:
  0.0 667.8 jit_solution(374609972447098960)
XLA Ops:
  27.8 4.7 fusion.101
  38.4 5.4 convolution_convert_fusion.7
  51.2 5.7 convolution_convert_fusion.6
  64.1 5.8 convolution_convert_fusion.5
  72.9 5.9 convolution_convert_fusion.4
  95.4 7.2 %collective-permute-done.4 = bf16[64,1536]{1,0:T(8,128)(2,1)} collective-permute-done((bf16[64,1536]{1,0:T(8,128)(2,1)}, bf16[64,1536]{1,0:T(8,128)(2,1)}, u32[]{:S(2)}, u32[]{:S(2)}) %collective-permute-start.4) | collective-permute-done | bytes 196640 | tf_op jit(solution)/shard_map/ppermute | solution.py:44
  107.1 4.1 multiply_convert_fusion.14
  121.2 4.5 collective-permute-done.7
  178.9 4.6 fusion.95
  197.6 20.1 %collective-permute-done.16 = bf16[64,1536]{1,0:T(8,128)(2,1)S(1)} collective-permute-done((bf16[64,1536]{1,0:T(8,128)(2,1)S(1)}, bf16[64,1536]{1,0:T(8,128)(2,1)S(1)}, u32[]{:S(2)}, u32[]{:S(2)}) %collective-permute-start.16) | collective-permute-done | bytes 196640 | tf_op jit(solution)/shard_map/ppermute | solution.py:44
  275.0 5.3 pad_maximum_fusion.1
  280.3 9.6 %copy.122 = f32[1536,1536]{1,0:T(8,128)} copy(f32[1536,1536]{0,1:T(8,128)} %pad_maximum_fusion.1) | data formatting | bytes 18874368 | tf_op jit(solution)/shard_map/concatenate | solution.py:234
  289.9 4.2 fusion.110
  302.0 5.3 collective-permute-done.19
  336.9 13.7 %collective-permute-done.46 = bf16[32,1536]{1,0:T(8,128)(2,1)} collective-permute-done((bf16[32,1536]{1,0:T(8,128)(2,1)}, bf16[32,1536]{1,0:T(8,128)(2,1)}, u32[]{:S(2)}, u32[]{:S(2)}) %collective-permute-start.46) | collective-permute-done | bytes 98336 | tf_op jit(solution)/shard_map/ppermute | solution.py:44
  422.7 5.3 pad_maximum_fusion
  428.0 9.9 %copy.121 = f32[1536,1536]{1,0:T(8,128)} copy(f32[1536,1536]{0,1:T(8,128)} %pad_maximum_fusion) | data formatting | bytes 18874368 | tf_op jit(solution)/shard_map/concatenate | solution.py:234
  438.0 4.2 fusion.109
  443.9 5.4 convolution_convert_fusion.2
  449.4 4.3 fusion.115
  469.1 4.9 collective-permute-done.28
  487.5 10.1 %fusion.38 = f32[1024,1536]{1,0:T(8,128)} fusion(bf16[1024,1536]{1,0:T(8,128)(2,1)} %constant_dynamic-update-slice_fusion.9, bf16[2,1536,1536]{2,1,0:T(8,128)(2,1)} %param.27), kind=kOutput, calls=%fused_computation.45 | convolution fusion | flops 4831838208 | bytes 14155776 | tf_op jit(solution)/shard_map/dot_general | solution.py:31
  501.6 11.6 %collective-permute-done.54 = bf16[256,1536]{1,0:T(8,128)(2,1)S(1)} collective-permute-done((bf16[256,1536]{1,0:T(8,128)(2,1)}, bf16[256,1536]{1,0:T(8,128)(2,1)S(1)}, u32[]{:S(2)}, u32[]{:S(2)}) %collective-permute-start.54) | collective-permute-done | bytes 786464 | tf_op jit(solution)/shard_map/ppermute | solution.py:44
  518.6 13.7 %collective-permute-done.44 = bf16[256,1536]{1,0:T(8,128)(2,1)S(1)} collective-permute-done((bf16[256,1536]{1,0:T(8,128)(2,1)S(1)}, bf16[256,1536]{1,0:T(8,128)(2,1)S(1)}, u32[]{:S(2)}, u32[]{:S(2)}) %collective-permute-start.44) | collective-permute-done | bytes 786464 | tf_op jit(solution)/shard_map/ppermute | solution.py:44
  536.0 5.5 add_convert_fusion
  541.5 17.6 %collective-permute-done.34 = bf16[2,192,1536]{2,1,0:T(8,128)(2,1)S(1)} collective-permute-done((bf16[2,192,1536]{2,1,0:T(8,128)(2,1)S(1)}, bf16[2,192,1536]{2,1,0:T(8,128)(2,1)S(1)}, u32[]{:S(2)}, u32[]{:S(2)}) %collective-permute-start.34) | collective-permute-done | bytes 1179680 | tf_op jit(solution)/shard_map/ppermute | solution.py:44
  565.7 8.1 %fusion.26 = f32[1024,1536]{1,0:T(8,128)S(1)} fusion(bf16[1024,1536]{1,0:T(8,128)(2,1)S(1)} %constant_dynamic-update-slice_fusion.31, bf16[2,1536,1536]{2,1,0:T(8,128)(2,1)} %param.27), kind=kOutput, calls=%fused_computation.35 | convolution fusion | flops 4831838208 | bytes 14155776 | tf_op jit(solution)/shard_map/dot_general | solution.py:31
  579.8 12.1 %convolution_bitcast_fusion.24 = f32[1,192,1536]{2,1,0:T(8,128)} fusion(f32[1024,1536]{1,0:T(8,128)} %copy-done.191, bf16[1024,1536]{1,0:T(8,128)(2,1)} %copy-done.185, bf16[2,1536,1536]{2,1,0:T(8,128)(2,1)} %param.28, bf16[1024,1536]{1,0:T(8,128)(2,1)} %copy-done.183, s32[]{:T(128)S(6)} %select_n.259), kind=kOutput, calls=%fused_computation.168 | convolution fusion | flops 5451546624 | bytes 15859716 | tf_op jit(solution)/shard_map/dot_general | solution.py:39
  594.6 12.3 %convolution_bitcast_fusion.25 = f32[1,192,1536]{2,1,0:T(8,128)} fusion(f32[1024,1536]{1,0:T(8,128)} %fusion.38, bf16[1024,1536]{1,0:T(8,128)(2,1)} %constant_dynamic-update-slice_fusion.20, bf16[2,1536,1536]{2,1,0:T(8,128)(2,1)} %param.28, bf16[1024,1536]{1,0:T(8,128)(2,1)} %constant_dynamic-update-slice_fusion.9, s32[]{:T(128)S(6)} %select_n.259), kind=kOutput, calls=%fused_computation.169 | convolution fusion | flops 5451546624 | bytes 15859716 | tf_op jit(solution)/shard_map/dot_general | solution.py:39
  606.9 5.2 fusion.87
  617.5 4.7 fusion.359
  643.4 21.1 %collective-permute-done.32 = bf16[1,192,1536]{2,1,0:T(8,128)(2,1)} collective-permute-done((bf16[1,192,1536]{2,1,0:T(8,128)(2,1)}, bf16[1,192,1536]{2,1,0:T(8,128)(2,1)}, u32[]{:S(2)}, u32[]{:S(2)}) %collective-permute-start.32) | collective-permute-done | bytes 589856 | tf_op jit(solution)/shard_map/ppermute | solution.py:44
  (837 shorter events, 402.1 us)
Async XLA Ops:
  0.7 44.5 %collective-permute-start = (bf16[2,256,1536]{2,1,0:T(8,128)(2,1)}, bf16[2,256,1536]{2,1,0:T(8,128)(2,1)}, u32[]{:S(2)}, u32[]{:S(2)}) collective-permute-start(bf16[2,256,1536]{2,1,0:T(8,128)(2,1)} %bitcast.523), channel_id=1, source_target_pairs={{0,1},{1,0},{2,3},{3,2},{4,5},{5,4},{6,7},{7,6},{8,9},{9,8},{10,11... | collective-permute-start | bytes 4718600 | tf_op jit(solution)/shard_map/ppermute | solution.py:44
  1.2 55.7 %collective-permute-start.1 = (bf16[2,256,1536]{2,1,0:T(8,128)(2,1)}, bf16[2,256,1536]{2,1,0:T(8,128)(2,1)}, u32[]{:S(2)}, u32[]{:S(2)}) collective-permute-start(bf16[2,256,1536]{2,1,0:T(8,128)(2,1)} %bitcast.524), channel_id=1, source_target_pairs={{0,2},{1,3},{2,0},{3,1},{4,6},{5,7},{6,4},{7,5},{8,10},{9,11},{10,... | collective-permute-start | bytes 4718600 | tf_op jit(solution)/shard_map/ppermute | solution.py:44
  166.8 24.1 %collective-permute-start.38 = (bf16[128,1536]{1,0:T(8,128)(2,1)}, bf16[128,1536]{1,0:T(8,128)(2,1)}, u32[]{:S(2)}, u32[]{:S(2)}) collective-permute-start(bf16[128,1536]{1,0:T(8,128)(2,1)} %pad_maximum_fusion.11), channel_id=1, source_target_pairs={{0,16},{4,20},{8,24},{12,28},{16,0},{20,4},{24,8},{28,12},{1,17},{... | collective-permute-start | bytes 1179656 | tf_op jit(solution)/shard_map/ppermute | solution.py:44
  192.9 114.6 %collective-permute-start.39 = (bf16[256,1536]{1,0:T(8,128)(2,1)}, bf16[256,1536]{1,0:T(8,128)(2,1)}, u32[]{:S(2)}, u32[]{:S(2)}) collective-permute-start(bf16[256,1536]{1,0:T(8,128)(2,1)} %pad_maximum_fusion.5), channel_id=1, source_target_pairs={{0,2},{1,3},{2,0},{3,1},{4,6},{5,7},{6,4},{7,5},{8,10},{9,11},{10,... | collective-permute-start | bytes 2359304 | tf_op jit(solution)/shard_map/ppermute | solution.py:44
  195.4 22.3 %collective-permute-start.16 = (bf16[64,1536]{1,0:T(8,128)(2,1)S(1)}, bf16[64,1536]{1,0:T(8,128)(2,1)S(1)}, u32[]{:S(2)}, u32[]{:S(2)}) collective-permute-start(bf16[64,1536]{1,0:T(8,128)(2,1)S(1)} %fusion.233), channel_id=1, source_target_pairs={{0,2},{1,3},{2,0},{3,1},{4,6},{5,7},{6,4},{7,5},{8,10},{9,11},{10,... | collective-permute-start | bytes 589832 | tf_op jit(solution)/shard_map/ppermute | solution.py:44
  197.0 24.1 %collective-permute-start.13 = (bf16[64,1536]{1,0:T(8,128)(2,1)S(1)}, bf16[64,1536]{1,0:T(8,128)(2,1)S(1)}, u32[]{:S(2)}, u32[]{:S(2)}) collective-permute-start(bf16[64,1536]{1,0:T(8,128)(2,1)S(1)} %fusion.234), channel_id=1, source_target_pairs={{0,2},{1,3},{2,0},{3,1},{4,6},{5,7},{6,4},{7,5},{8,10},{9,11},{10,... | collective-permute-start | bytes 589832 | tf_op jit(solution)/shard_map/ppermute | solution.py:44
  221.8 75.6 %collective-permute-start.14 = (bf16[64,1536]{1,0:T(8,128)(2,1)}, bf16[64,1536]{1,0:T(8,128)(2,1)}, u32[]{:S(2)}, u32[]{:S(2)}) collective-permute-start(bf16[64,1536]{1,0:T(8,128)(2,1)} %add_convert_fusion.5), channel_id=1, source_target_pairs={{0,1},{1,0},{2,3},{3,2},{4,5},{5,4},{6,7},{7,6},{8,9},{9,8},{10,11... | collective-permute-start | bytes 589832 | tf_op jit(solution)/shard_map/ppermute | solution.py:44
  258.0 41.7 %collective-permute-start.18 = (bf16[64,1536]{1,0:T(8,128)(2,1)}, bf16[64,1536]{1,0:T(8,128)(2,1)}, u32[]{:S(2)}, u32[]{:S(2)}) collective-permute-start(bf16[64,1536]{1,0:T(8,128)(2,1)} %fusion.249), channel_id=1, source_target_pairs={{0,1},{1,0},{2,3},{3,2},{4,5},{5,4},{6,7},{7,6},{8,9},{9,8},{10,11... | collective-permute-start | bytes 589832 | tf_op jit(solution)/shard_map/ppermute | solution.py:44
  294.1 220.4 %collective-permute-start.33 = (bf16[4,192,1536]{2,1,0:T(8,128)(2,1)}, bf16[4,192,1536]{2,1,0:T(8,128)(2,1)}, u32[]{:S(2)}, u32[]{:S(2)}) collective-permute-start(bf16[4,192,1536]{2,1,0:T(8,128)(2,1)} %fusion.110), channel_id=1, source_target_pairs={{0,4},{4,0},{8,12},{12,8},{16,20},{20,16},{24,28},{28,24},{1,5},{5... | collective-permute-start | bytes 7077896 | tf_op jit(solution)/shard_map/ppermute | solution.py:44
  309.9 173.0 %collective-permute-start.40 = (bf16[512,1536]{1,0:T(8,128)(2,1)}, bf16[512,1536]{1,0:T(8,128)(2,1)}, u32[]{:S(2)}, u32[]{:S(2)}) collective-permute-start(bf16[512,1536]{1,0:T(8,128)(2,1)} %get-tuple-element.99), channel_id=1, source_target_pairs={{0,1},{1,0},{2,3},{3,2},{4,5},{5,4},{6,7},{7,6},{8,9},{9,8},{10,11... | collective-permute-start | bytes 4718600 | tf_op jit(solution)/shard_map/ppermute | solution.py:44
  318.5 32.1 %collective-permute-start.46 = (bf16[32,1536]{1,0:T(8,128)(2,1)}, bf16[32,1536]{1,0:T(8,128)(2,1)}, u32[]{:S(2)}, u32[]{:S(2)}) collective-permute-start(bf16[32,1536]{1,0:T(8,128)(2,1)} %get-tuple-element.96), channel_id=1, source_target_pairs={{0,4},{4,0},{8,12},{12,8},{16,20},{20,16},{24,28},{28,24},{1,5},{5... | collective-permute-start | bytes 294920 | tf_op jit(solution)/shard_map/ppermute | solution.py:44
  320.6 32.1 %collective-permute-start.51 = (bf16[32,1536]{1,0:T(8,128)(2,1)}, bf16[32,1536]{1,0:T(8,128)(2,1)}, u32[]{:S(2)}, u32[]{:S(2)}) collective-permute-start(bf16[32,1536]{1,0:T(8,128)(2,1)} %get-tuple-element.98), channel_id=1, source_target_pairs={{0,4},{4,0},{8,12},{12,8},{16,20},{20,16},{24,28},{28,24},{1,5},{5... | collective-permute-start | bytes 294920 | tf_op jit(solution)/shard_map/ppermute | solution.py:44
  335.7 19.6 %collective-permute-start.41 = (bf16[32,1536]{1,0:T(8,128)(2,1)S(1)}, bf16[32,1536]{1,0:T(8,128)(2,1)S(1)}, u32[]{:S(2)}, u32[]{:S(2)}) collective-permute-start(bf16[32,1536]{1,0:T(8,128)(2,1)S(1)} %get-tuple-element.34), channel_id=1, source_target_pairs={{0,4},{4,0},{8,12},{12,8},{16,20},{20,16},{24,28},{28,24},{1,5},{5... | collective-permute-start | bytes 294920 | tf_op jit(solution)/shard_map/ppermute | solution.py:44
  362.2 11.4 %collective-permute-start.22 = (bf16[64,1536]{1,0:T(8,128)(2,1)S(1)}, bf16[64,1536]{1,0:T(8,128)(2,1)S(1)}, u32[]{:S(2)}, u32[]{:S(2)}) collective-permute-start(bf16[64,1536]{1,0:T(8,128)(2,1)S(1)} %fusion.231), channel_id=1, source_target_pairs={{0,2},{1,3},{2,0},{3,1},{4,6},{5,7},{6,4},{7,5},{8,10},{9,11},{10,... | collective-permute-start | bytes 589832 | tf_op jit(solution)/shard_map/ppermute | solution.py:44
  364.8 93.3 %collective-permute-start.48 = (bf16[128,1536]{1,0:T(8,128)(2,1)}, bf16[128,1536]{1,0:T(8,128)(2,1)}, u32[]{:S(2)}, u32[]{:S(2)}) collective-permute-start(bf16[128,1536]{1,0:T(8,128)(2,1)} %pad_maximum_fusion.13), channel_id=1, source_target_pairs={{0,16},{4,20},{8,24},{12,28},{16,0},{20,4},{24,8},{28,12},{1,17},{... | collective-permute-start | bytes 1179656 | tf_op jit(solution)/shard_map/ppermute | solution.py:44
  369.1 91.3 %collective-permute-start.53 = (bf16[128,1536]{1,0:T(8,128)(2,1)}, bf16[128,1536]{1,0:T(8,128)(2,1)}, u32[]{:S(2)}, u32[]{:S(2)}) collective-permute-start(bf16[128,1536]{1,0:T(8,128)(2,1)} %pad_maximum_fusion.14), channel_id=1, source_target_pairs={{0,16},{4,20},{8,24},{12,28},{16,0},{20,4},{24,8},{28,12},{1,17},{... | collective-permute-start | bytes 1179656 | tf_op jit(solution)/shard_map/ppermute | solution.py:44
  375.1 87.6 %collective-permute-start.43 = (bf16[128,1536]{1,0:T(8,128)(2,1)}, bf16[128,1536]{1,0:T(8,128)(2,1)}, u32[]{:S(2)}, u32[]{:S(2)}) collective-permute-start(bf16[128,1536]{1,0:T(8,128)(2,1)} %pad_maximum_fusion.12), channel_id=1, source_target_pairs={{0,16},{4,20},{8,24},{12,28},{16,0},{20,4},{24,8},{28,12},{1,17},{... | collective-permute-start | bytes 1179656 | tf_op jit(solution)/shard_map/ppermute | solution.py:44
  458.1 76.7 %collective-permute-start.25 = (bf16[512,1536]{1,0:T(8,128)(2,1)}, bf16[512,1536]{1,0:T(8,128)(2,1)}, u32[]{:S(2)}, u32[]{:S(2)}) collective-permute-start(bf16[512,1536]{1,0:T(8,128)(2,1)} %convolution_convert_fusion.2), channel_id=1, source_target_pairs={{0,1},{1,0},{2,3},{3,2},{4,5},{5,4},{6,7},{7,6},{8,9},{9,8},{10,11... | collective-permute-start | bytes 4718600 | tf_op jit(solution)/shard_map/ppermute | solution.py:44
  460.5 157.0 %collective-permute-start.24 = (bf16[512,1536]{1,0:T(8,128)(2,1)}, bf16[512,1536]{1,0:T(8,128)(2,1)}, u32[]{:S(2)}, u32[]{:S(2)}) collective-permute-start(bf16[512,1536]{1,0:T(8,128)(2,1)} %convolution_convert_fusion.3), channel_id=1, source_target_pairs={{0,1},{1,0},{2,3},{3,2},{4,5},{5,4},{6,7},{7,6},{8,9},{9,8},{10,11... | collective-permute-start | bytes 4718600 | tf_op jit(solution)/shard_map/ppermute | solution.py:44
  476.2 21.4 %collective-permute-start.49 = (bf16[256,1536]{1,0:T(8,128)(2,1)}, bf16[256,1536]{1,0:T(8,128)(2,1)}, u32[]{:S(2)}, u32[]{:S(2)}) collective-permute-start(bf16[256,1536]{1,0:T(8,128)(2,1)} %pad_maximum_fusion.7), channel_id=1, source_target_pairs={{0,2},{1,3},{2,0},{3,1},{4,6},{5,7},{6,4},{7,5},{8,10},{9,11},{10,... | collective-permute-start | bytes 2359304 | tf_op jit(solution)/shard_map/ppermute | solution.py:44
  482.9 30.3 %collective-permute-start.54 = (bf16[256,1536]{1,0:T(8,128)(2,1)}, bf16[256,1536]{1,0:T(8,128)(2,1)S(1)}, u32[]{:S(2)}, u32[]{:S(2)}) collective-permute-start(bf16[256,1536]{1,0:T(8,128)(2,1)} %pad_maximum_fusion.8), channel_id=1, source_target_pairs={{0,2},{1,3},{2,0},{3,1},{4,6},{5,7},{6,4},{7,5},{8,10},{9,11},{10,... | collective-permute-start | bytes 2359304 | tf_op jit(solution)/shard_map/ppermute | solution.py:44
  497.6 62.8 %collective-permute-start.30 = (bf16[4,192,1536]{2,1,0:T(8,128)(2,1)S(1)}, bf16[4,192,1536]{2,1,0:T(8,128)(2,1)S(1)}, u32[]{:S(2)}, u32[]{:S(2)}) collective-permute-start(bf16[4,192,1536]{2,1,0:T(8,128)(2,1)S(1)} %copy-done.86), channel_id=1, source_target_pairs={{0,4},{4,0},{8,12},{12,8},{16,20},{20,16},{24,28},{28,24},{1,5},{5... | collective-permute-start | bytes 7077896 | tf_op jit(solution)/shard_map/ppermute | solution.py:44
  513.2 19.2 %collective-permute-start.44 = (bf16[256,1536]{1,0:T(8,128)(2,1)S(1)}, bf16[256,1536]{1,0:T(8,128)(2,1)S(1)}, u32[]{:S(2)}, u32[]{:S(2)}) collective-permute-start(bf16[256,1536]{1,0:T(8,128)(2,1)S(1)} %copy-done.137), channel_id=1, source_target_pairs={{0,2},{1,3},{2,0},{3,1},{4,6},{5,7},{6,4},{7,5},{8,10},{9,11},{10,... | collective-permute-start | bytes 2359304 | tf_op jit(solution)/shard_map/ppermute | solution.py:44
  515.6 47.6 %collective-permute-start.50 = (bf16[512,1536]{1,0:T(8,128)(2,1)}, bf16[512,1536]{1,0:T(8,128)(2,1)S(1)}, u32[]{:S(2)}, u32[]{:S(2)}) collective-permute-start(bf16[512,1536]{1,0:T(8,128)(2,1)} %get-tuple-element.103), channel_id=1, source_target_pairs={{0,1},{1,0},{2,3},{3,2},{4,5},{5,4},{6,7},{7,6},{8,9},{9,8},{10,11... | collective-permute-start | bytes 4718600 | tf_op jit(solution)/shard_map/ppermute | solution.py:44
  532.3 26.7 %collective-permute-start.34 = (bf16[2,192,1536]{2,1,0:T(8,128)(2,1)S(1)}, bf16[2,192,1536]{2,1,0:T(8,128)(2,1)S(1)}, u32[]{:S(2)}, u32[]{:S(2)}) collective-permute-start(bf16[2,192,1536]{2,1,0:T(8,128)(2,1)S(1)} %fusion.148), channel_id=1, source_target_pairs={{0,8},{4,12},{8,0},{12,4},{16,24},{20,28},{24,16},{28,20},{1,9},{5... | collective-permute-start | bytes 3538952 | tf_op jit(solution)/shard_map/ppermute | solution.py:44
  534.8 39.1 %collective-permute-start.55 = (bf16[512,1536]{1,0:T(8,128)(2,1)}, bf16[512,1536]{1,0:T(8,128)(2,1)S(1)}, u32[]{:S(2)}, u32[]{:S(2)}) collective-permute-start(bf16[512,1536]{1,0:T(8,128)(2,1)} %copy-done.178), channel_id=1, source_target_pairs={{0,1},{1,0},{2,3},{3,2},{4,5},{5,4},{6,7},{7,6},{8,9},{9,8},{10,11... | collective-permute-start | bytes 4718600 | tf_op jit(solution)/shard_map/ppermute | solution.py:44
  559.0 32.9 %collective-permute-start.45 = (bf16[512,1536]{1,0:T(8,128)(2,1)}, bf16[512,1536]{1,0:T(8,128)(2,1)}, u32[]{:S(2)}, u32[]{:S(2)}) collective-permute-start(bf16[512,1536]{1,0:T(8,128)(2,1)} %copy-done.176), channel_id=1, source_target_pairs={{0,1},{1,0},{2,3},{3,2},{4,5},{5,4},{6,7},{7,6},{8,9},{9,8},{10,11... | collective-permute-start | bytes 4718600 | tf_op jit(solution)/shard_map/ppermute | solution.py:44
  561.0 56.5 %collective-permute-start.26 = (bf16[512,1536]{1,0:T(8,128)(2,1)}, bf16[512,1536]{1,0:T(8,128)(2,1)}, u32[]{:S(2)}, u32[]{:S(2)}) collective-permute-start(bf16[512,1536]{1,0:T(8,128)(2,1)} %add_convert_fusion), channel_id=1, source_target_pairs={{0,2},{1,3},{2,0},{3,1},{4,6},{5,7},{6,4},{7,5},{8,10},{9,11},{10,... | collective-permute-start | bytes 4718600 | tf_op jit(solution)/shard_map/ppermute | solution.py:44
  563.3 52.0 %collective-permute-start.35 = (bf16[1,192,1536]{2,1,0:T(8,128)(2,1)}, bf16[1,192,1536]{2,1,0:T(8,128)(2,1)}, u32[]{:S(2)}, u32[]{:S(2)}) collective-permute-start(bf16[1,192,1536]{2,1,0:T(8,128)(2,1)} %dynamic-slice_convert_fusion.3), channel_id=1, source_target_pairs={{0,16},{4,20},{8,24},{12,28},{16,0},{20,4},{24,8},{28,12},{1,17},{... | collective-permute-start | bytes 1769480 | tf_op jit(solution)/shard_map/ppermute | solution.py:44
  573.9 56.5 %collective-permute-start.31 = (bf16[2,192,1536]{2,1,0:T(8,128)(2,1)}, bf16[2,192,1536]{2,1,0:T(8,128)(2,1)}, u32[]{:S(2)}, u32[]{:S(2)}) collective-permute-start(bf16[2,192,1536]{2,1,0:T(8,128)(2,1)} %fusion.147), channel_id=1, source_target_pairs={{0,8},{4,12},{8,0},{12,4},{16,24},{20,28},{24,16},{28,20},{1,9},{5... | collective-permute-start | bytes 3538952 | tf_op jit(solution)/shard_map/ppermute | solution.py:44
  626.7 13.8 %all-to-all-start = ((f32[32,1,1056]{2,1,0:T(1,128)}), f32[32,1,1056]{2,1,0:T(1,128)S(1)}, u32[]{:S(2)}, u32[]{:S(2)}) async-start(f32[32,1,1056]{2,1,0:T(1,128)} %all_to_all.6), calls=%async_computation | async-start | bytes 294912 | tf_op jit(solution)/shard_map/all_to_all | solution.py:256
  635.2 29.3 %collective-permute-start.32 = (bf16[1,192,1536]{2,1,0:T(8,128)(2,1)}, bf16[1,192,1536]{2,1,0:T(8,128)(2,1)}, u32[]{:S(2)}, u32[]{:S(2)}) collective-permute-start(bf16[1,192,1536]{2,1,0:T(8,128)(2,1)} %dynamic-slice_convert_fusion.4), channel_id=1, source_target_pairs={{0,16},{4,20},{8,24},{12,28},{16,0},{20,4},{24,8},{28,12},{1,17},{... | collective-permute-start | bytes 1769480 | tf_op jit(solution)/shard_map/ppermute | solution.py:44
  (231 other events, 1423.9 us)
